TPU v7x, 32 devices: a whole 2x2x4 slice. The times are simulated.
32 devices in a mesh: grp: 4 (over y, x), dev: 8 (over z, core).
Axes of the slice: x: 2, y: 2, z: 4, core: 2. Of those that a mesh axis runs over, the one named last changes fastest.
Arguments:
- ref_volume: bfloat16 [256, 128, 1024], P('dev', None, 'grp'), may hold values from -6 to 6
- def_volume: bfloat16 [256, 128, 1024], P('dev', None, 'grp'), may hold values from -6 to 6
- shifts: int32 [4, 8], P('grp', 'dev'), may hold values from -8 to 8, as said below
- init_disp: float32 [3, 17, 9, 65], replicated, may hold values from -3 to 3
- precond: float32 [3, 17, 9, 65], replicated, may hold values from 0.001 to 0.01
Outputs:
- displacement: float32 [3, 17, 9, 65], replicated
- residual: float32 [256, 128, 1024], P('dev', None, 'grp')
- misfit: float32 [], replicated
Inputs may be any that keep to these rules, and one draw needn't show every extreme that they name: `shifts`: every entry lies within 8 in magnitude; both 8 and -8 occur in every draw.
All inputs are finite; a program needn't handle non-finite values.
Results may differ from a plain program's by a relative error of at most 0.0003.
Values may be sent and summed in bfloat16 or wider, within the bound.
A program may use at most 128 MiB of HBM per device.

v0:
```python
import jax
import jax.numpy as jnp
from jax import lax
from jax.sharding import PartitionSpec as P

E = 16
SMAX = 8
ITERS = 2


epsilon = 1e-06


def with_halo(shard, sides, width):
    for axis, dim in sides:
        devices, length = (lax.axis_size(axis), shard.shape[dim])
        up = [(i, (i + 1) % devices) for i in range(devices - 1)]
        down = [(j, i) for i, j in up]
        last = lax.slice_in_dim(shard, length - width, length, axis=dim)
        initial = lax.slice_in_dim(shard, 0, width, axis=dim)
        before = lax.ppermute(last, axis, up)
        after = lax.ppermute(initial, axis, down)
        shard = jnp.concatenate([before, shard, after], axis=dim)
    return shard


def hat_matrix(voxels, nodes):
    positions = jnp.arange(voxels, dtype=jnp.int32)
    element = positions // E
    fraction = (positions - element * E).astype(jnp.float32) / E
    columns = jnp.arange(nodes, dtype=jnp.int32)
    left_part = (columns[None, :] == element[:, None]).astype(jnp.float32) * (1.0 - fraction)[
        :, None
    ]
    right_part = (columns[None, :] == element[:, None] + 1).astype(jnp.float32) * fraction[:, None]
    return left_part + right_part


def smooth(values, direction):
    extent = values.shape[direction]
    lower = lax.slice_in_dim(values, 0, extent - 2, axis=direction)
    middle = lax.slice_in_dim(values, 1, extent - 1, axis=direction)
    upper = lax.slice_in_dim(values, 2, extent, axis=direction)
    return (lower + 4.0 * middle + upper) / 6.0


def differ(values, direction):
    extent = values.shape[direction]
    lower = lax.slice_in_dim(values, 0, extent - 2, axis=direction)
    upper = lax.slice_in_dim(values, 2, extent, axis=direction)
    return 0.5 * (upper - lower)


def gradients(window):
    smooth_z = smooth(window, 2)
    slope_x = differ(smooth(smooth_z, 1), 0)
    slope_y = smooth(differ(smooth_z, 1), 0)
    slope_z = smooth(smooth(differ(window, 2), 1), 0)
    return jnp.stack([slope_x, slope_y, slope_z])


def interpolate(local_nodes, hat_x, hat_y, hat_z):
    highest = lax.Precision.HIGHEST
    partial_z = jnp.einsum("cijk,zk->cijz", local_nodes, hat_z, precision=highest)
    partial_y = jnp.einsum("cijz,yj->ciyz", partial_z, hat_y, precision=highest)
    return jnp.einsum("ciyz,xi->cxyz", partial_y, hat_x, precision=highest)


def restrict(terms, hat_x, hat_y, hat_z):
    highest = lax.Precision.HIGHEST
    partial_x = jnp.einsum("cxyz,xi->ciyz", terms, hat_x, precision=highest)
    partial_y = jnp.einsum("ciyz,yj->cijz", partial_x, hat_y, precision=highest)
    return jnp.einsum("cijz,zk->cijk", partial_y, hat_z, precision=highest)


def local(ref_volume, def_volume, shifts, init_disp, precond):
    width_x, rows_y, depth_z = ref_volume.shape
    dev_count = lax.axis_size("dev")
    grp_count = lax.axis_size("grp")
    grp_index = lax.axis_index("grp")
    dev_index = lax.axis_index("dev")
    voxel_count = float(width_x * rows_y * depth_z * dev_count * grp_count)
    margin = SMAX + 1
    offset = shifts[0, 0]
    widened = with_halo(def_volume, (("dev", 0),), margin)
    framed = with_halo(widened, (("grp", 2),), 1)
    window = lax.dynamic_slice_in_dim(framed, offset + margin - 1, width_x + 2, 0)
    window = jnp.pad(window, ((0, 0), (1, 1), (0, 0))).astype(jnp.float32)
    slopes = gradients(window)
    sample = window[1:-1, 1:-1, 1:-1]
    target = ref_volume.astype(jnp.float32)
    elements_x = width_x // E
    elements_z = depth_z // E
    nodes_y = rows_y // E + 1
    nodes_x = elements_x * dev_count + 1
    nodes_z = elements_z * grp_count + 1
    hat_x = hat_matrix(width_x, elements_x + 1)
    hat_y = hat_matrix(rows_y, nodes_y)
    hat_z = hat_matrix(depth_z, elements_z + 1)
    motion = init_disp
    fixed_sums = lax.psum((jnp.sum(target), jnp.sum(target * target)), ("grp", "dev"))
    mean_ref = fixed_sums[0] / voxel_count
    var_ref = fixed_sums[1] / voxel_count - mean_ref * mean_ref
    residual = target
    totals = None
    for iteration in range(ITERS):
        corner = (0, dev_index * elements_x, 0, grp_index * elements_z)
        local_nodes = lax.dynamic_slice(
            motion, corner, (3, elements_x + 1, nodes_y, elements_z + 1)
        )
        shift_field = interpolate(local_nodes, hat_x, hat_y, hat_z)
        warped = sample + jnp.sum(shift_field * slopes, axis=0)
        image_sums = lax.psum((jnp.sum(warped), jnp.sum(warped * warped)), ("grp", "dev"))
        mean_img = image_sums[0] / voxel_count
        var_img = image_sums[1] / voxel_count - mean_img * mean_img
        ratio = jnp.sqrt((var_ref + epsilon) / (var_img + epsilon))
        residual = target - mean_ref - ratio * (warped - mean_img)
        slab = restrict(slopes * residual[None], hat_x, hat_y, hat_z)
        slab_stack = slab[None]
        kinds = slab_stack.shape[0]
        whole = jnp.zeros((kinds, 3, nodes_x, nodes_y, nodes_z), jnp.float32)
        whole = lax.dynamic_update_slice(
            whole, slab_stack, (0, 0, dev_index * elements_x, 0, grp_index * elements_z)
        )
        forces, totals = lax.psum((whole, jnp.sum(residual * residual)[None]), ("grp", "dev"))
        motion = motion + precond * forces[0]
    misfit = jnp.sqrt(totals[0] / voxel_count)
    return (motion, residual, misfit)


def solution(mesh):
    placed = (P("dev", None, "grp"), P("dev", None, "grp"), P("grp", "dev"), P(), P())
    return jax.shard_map(
        local,
        mesh=mesh,
        in_specs=placed,
        out_specs=(P(), P("dev", None, "grp"), P()),
        check_vma=False,
    )
```

profile of v0, /device:TPU:1, one launch (start us, length us, event | category | flops | bytes accessed | tf_op | source)
XLA Modules:
  0.0 522.8 jit_solution(11183667305458659384)
XLA Ops:
  9.5 4.6 collective-permute-start
  32.7 3.8 copy.18
  36.6 3.1 collective-permute-start.2
  39.7 3.7 copy.19
  45.6 3.9 copy.20
  49.4 3.8 copy.21
  53.3 8.6 %fusion.28 = bf16[34,128,258]{2,0,1:T(8,128)(2,1)S(1)} fusion(s32[]{:T(128)S(6)} %select_n.89, bf16[50,128,1]{2,0,1:T(8,128)(2,1)} %copy.20, bf16[9,128,256]{2,0,1:T(8,128)(2,1)S(1)} %copy.15, bf16[32,128,256]{2,0,1:T(8,128)(2,1)S(1)} %copy-done.12, bf16[9,128,256]{2,0,1:T(8,128)(2,1)} %copy-done.15, bf16[50,128,1]{2,0,1:T(8,128)(2,1)} %copy.21), kind=kLoop, calls=%fused_computation.56 | loop fusion | flops 11228160 | bytes 5548036 | tf_op jit(solution)/shard_map/concatenate | solution.py:23
  62.5 2.9 fusion.10
  65.4 4.7 fusion.15
  70.1 3.0 fusion.11
  73.1 5.0 fusion.26
  78.4 11.1 %fusion.20 = (f32[1,32,128,256]{3,1,2,0:T(8,128)}, f32[1,32,128,256]{3,1,2,0:T(8,128)}) fusion(f32[34,128,256]{2,0,1:T(8,128)S(1)} %bitcast.80, f32[34,128,256]{2,0,1:T(8,128)} %get-tuple-element.26), kind=kLoop, calls=%fused_computation.38 | loop fusion | flops 8388608 | bytes 33554432 | tf_op jit(solution)/shard_map/stack | solution.py:59
  89.5 15.3 %fusion.1 = f32[32,128,256]{2,0,1:T(8,128)S(1)} fusion(f32[128,3,3,256]{3,0,2,1:T(8,128)S(1)} %copy-done.19, f32[1,32,128,256]{3,1,2,0:T(8,128)} %get-tuple-element.41, f32[1,32,128,256]{3,1,2,0:T(8,128)} %get-tuple-element.42, f32[1,32,128,256]{3,1,2,0:T(8,128)S(1)} %fusion.26, f32[32]{0:T(128)S(1)} %convert_multiply_fusion.2, ...), kind=kOutput, calls=%fused_computation.4 | convolution fusion | flops 124781024 | bytes 17957376 | tf_op jit(solution)/shard_map/ciyz,xi->cxyz/dot_general | solution.py:66
  106.9 41.5 %all-reduce.2 = (f32[]{:T(128)}, f32[]{:T(128)}, f32[]{:T(128)}, f32[]{:T(128)}) all-reduce(f32[]{:T(128)} %get-tuple-element.12, f32[]{:T(128)} %get-tuple-element.14, f32[]{:T(128)} %get-tuple-element.13, f32[]{:T(128)} %get-tuple-element.11), channel_id=1, replica_groups=mesh['grp'=4,'dev'=8] {'grp','dev'}, use_global_device_ids=true, to_apply=%region_8.9 | all-reduce | flops 4 | bytes 32 | tf_op jit(solution)/shard_map/psum | solution.py:113
  153.5 7.2 %fusion.17 = f32[32,128,256]{2,0,1:T(8,128)S(1)} fusion(f32[]{:T(128)S(6)} %div.145, f32[]{:T(128)S(6)} %sqrt.12, f32[]{:T(128)S(6)} %div.137, bf16[32,128,256]{2,1,0:T(8,128)(2,1)S(1)} %copy-done.10, f32[32,128,256]{2,0,1:T(8,128)} %copy-done.13, f32[34,130,258]{2,0,1:T(8,128)} %copy-done), kind=kLoop, calls=%fused_computation.34 | loop fusion | flops 6291456 | bytes 14680076 | tf_op jit(solution)/shard_map/sub | solution.py:117
  161.6 6.5 %fusion.4 = f32[3,3,128,256]{3,0,2,1:T(4,128)S(1)} fusion(f32[32,128,256]{2,0,1:T(8,128)S(1)} %fusion.17, f32[1,32,128,256]{3,1,2,0:T(8,128)S(1)} %copy-done.5, f32[1,32,128,256]{3,1,2,0:T(8,128)S(1)} %copy-done.7, f32[1,32,128,256]{3,1,2,0:T(8,128)S(1)} %copy-done.3, f32[32]{0:T(128)S(1)} %convert_multiply_fusion.2, s32[32]{0:T(128)S(1)} %get-tuple-element.34, ...), kind=kOutput, calls=%fused_computation.7 | convolution fusion | flops 122683872 | bytes 17957376 | tf_op jit(solution)/shard_map/cxyz,xi->ciyz/dot_general | solution.py:71
  170.8 130.6 %all-reduce.6.cloned.1.call-done = f32[3,17,9,65]{3,0,2,1:T(4,128)} async-done(((f32[3,17,9,65]{3,0,2,1:T(4,128)}), f32[3,17,9,65]{3,0,2,1:T(4,128)}) %all-reduce.6.cloned.1.call-update) | async-done | bytes 119356 | tf_op jit(solution)/shard_map/psum | solution.py:125
  304.3 15.4 %fusion = f32[32,128,256]{2,0,1:T(8,128)S(1)} fusion(f32[128,3,3,256]{3,0,2,1:T(8,128)S(1)} %fusion.52, f32[1,32,128,256]{3,1,2,0:T(8,128)} %get-tuple-element.41, f32[1,32,128,256]{3,1,2,0:T(8,128)} %get-tuple-element.42, f32[1,32,128,256]{3,1,2,0:T(8,128)} %copy-done.2, f32[32]{0:T(128)S(1)} %convert_multiply_fusion.2, s32[32]{0:T(128)S(1)} %get-tuple-element.34, ...), kind=kOutput, calls=%fused_computation.2 | convolution fusion | flops 124781024 | bytes 17957376 | tf_op jit(solution)/shard_map/ciyz,xi->cxyz/dot_general | solution.py:66
  321.8 41.0 %all-reduce.1 = (f32[]{:T(128)}, f32[]{:T(128)}) all-reduce(f32[]{:T(128)} %get-tuple-element.10, f32[]{:T(128)} %get-tuple-element.9), channel_id=1, replica_groups=mesh['grp'=4,'dev'=8] {'grp','dev'}, use_global_device_ids=true, to_apply=%region_14.15 | all-reduce | flops 2 | bytes 16 | tf_op jit(solution)/shard_map/psum | solution.py:113
  365.5 8.0 %multiply_reduce_fusion = (f32[]{:T(128)}, f32[32,128,256]{2,0,1:T(8,128)S(1)}) fusion(f32[]{:T(128)S(6)} %div.148, f32[32,128,256]{2,0,1:T(8,128)} %copy-done.14, f32[34,130,258]{2,0,1:T(8,128)} %copy-done, f32[]{:T(128)S(6)} %sqrt.13, f32[]{:T(128)S(6)} %div.137, bf16[32,128,256]{2,1,0:T(8,128)(2,1)S(1)} %copy-done.10), kind=kLoop, calls=%fused_computation.49 | loop fusion | flops 8388607 | bytes 14680080 | tf_op jit(solution)/shard_map/reduce_sum | solution.py:125
  373.6 6.5 %fusion.2 = f32[3,3,128,256]{3,0,2,1:T(4,128)S(1)} fusion(f32[32,128,256]{2,0,1:T(8,128)S(1)} %get-tuple-element.22, f32[1,32,128,256]{3,1,2,0:T(8,128)S(1)} %copy-done.6, f32[1,32,128,256]{3,1,2,0:T(8,128)S(1)} %copy-done.8, f32[1,32,128,256]{3,1,2,0:T(8,128)S(1)} %copy-done.4, f32[32]{0:T(128)S(1)} %convert_multiply_fusion.2, ...), kind=kOutput, calls=%fused_computation.5 | convolution fusion | flops 122683872 | bytes 17957376 | tf_op jit(solution)/shard_map/cxyz,xi->ciyz/dot_general | solution.py:71
  382.6 44.8 %psum.71 = f32[1]{0:T(128)} all-reduce(f32[1]{0:T(128)} %bitcast.24), channel_id=1, replica_groups=mesh['grp'=4,'dev'=8] {'grp','dev'}, use_global_device_ids=true, to_apply=%region_17.18 | all-reduce | flops 1 | bytes 8 | tf_op jit(solution)/shard_map/psum | solution.py:125
  427.4 6.7 %copy.25 = f32[32,128,256]{2,1,0:T(8,128)} copy(f32[32,128,256]{2,0,1:T(8,128)} %copy-done.1) | data formatting | bytes 8388608
  434.7 77.9 %all-reduce.8.cloned.1.call-done = f32[3,17,9,65]{3,0,2,1:T(4,128)} async-done(((f32[3,17,9,65]{3,0,2,1:T(4,128)}), f32[3,17,9,65]{3,0,2,1:T(4,128)}) %all-reduce.8.cloned.1.call-update) | async-done | bytes 119356 | tf_op jit(solution)/shard_map/psum | solution.py:125
  (95 shorter events, 38.1 us)
Async XLA Ops:
  7.2 15.1 %copy-start.9 = (bf16[32,128,256]{2,1,0:T(8,128)(2,1)S(1)}, bf16[32,128,256]{2,1,0:T(8,128)(2,1)}, u32[]{:S(2)}) copy-start(bf16[32,128,256]{2,1,0:T(8,128)(2,1)} %param.5) | copy-start | bytes 6291460
  7.2 294.3 %all-reduce.6.cloned.1.call-start = ((), (), s32[]{:S(2)}) async-start(), calls=%async_computation | async-start | bytes 626688 | tf_op jit(solution)/shard_map/psum | solution.py:125
  9.5 14.5 %collective-permute-start = (bf16[9,128,256]{2,1,0:T(8,128)(2,1)S(1)}, bf16[9,128,256]{2,1,0:T(8,128)(2,1)}, u32[]{:S(2)}, u32[]{:S(2)}) collective-permute-start(bf16[9,128,256]{2,1,0:T(8,128)(2,1)S(1)} %get-tuple-element.29), channel_id=1, source_target_pairs={{0,1},{1,2},{2,3},{3,4},{4,5},{5,6},{6,7},{8,9},{9,10},{10,11},{11... | collective-permute-start | bytes 1769480 | tf_op jit(solution)/shard_map/ppermute | solution.py:21
  14.1 11.5 %collective-permute-start.1 = (bf16[9,128,256]{2,1,0:T(8,128)(2,1)}, bf16[9,128,256]{2,1,0:T(8,128)(2,1)}, u32[]{:S(2)}, u32[]{:S(2)}) collective-permute-start(bf16[9,128,256]{2,1,0:T(8,128)(2,1)} %get-tuple-element.30), channel_id=1, source_target_pairs={{1,0},{2,1},{3,2},{4,3},{5,4},{6,5},{7,6},{9,8},{10,9},{11,10},{12... | collective-permute-start | bytes 1769480 | tf_op jit(solution)/shard_map/ppermute | solution.py:22
  20.1 7.0 %copy-start.11 = (bf16[32,128,256]{2,0,1:T(8,128)(2,1)}, bf16[32,128,256]{2,0,1:T(8,128)(2,1)S(1)}, u32[]{:S(2)}) copy-start(bf16[32,128,256]{2,0,1:T(8,128)(2,1)S(1)} %copy.16) | copy-start | bytes 6291460
  32.7 20.6 %copy-start.12 = (bf16[32,128,256]{2,0,1:T(8,128)(2,1)S(1)}, bf16[32,128,256]{2,0,1:T(8,128)(2,1)}, u32[]{:S(2)}) copy-start(bf16[32,128,256]{2,0,1:T(8,128)(2,1)} %copy-done.11) | copy-start | bytes 6291460
  36.6 9.0 %collective-permute-start.2 = (bf16[50,128,1]{1,0,2:T(8,128)(2,1)S(1)}, bf16[50,128,1]{1,0,2:T(8,128)(2,1)S(1)}, u32[]{:S(2)}, u32[]{:S(2)}) collective-permute-start(bf16[50,128,1]{1,0,2:T(8,128)(2,1)S(1)} %copy.18), channel_id=1, source_target_pairs={{0,8},{8,16},{16,24},{1,9},{9,17},{17,25},{2,10},{10,18},{18,26},{... | collective-permute-start | bytes 38408 | tf_op jit(solution)/shard_map/ppermute | solution.py:21
  43.4 6.0 %collective-permute-start.3 = (bf16[50,128,1]{1,0,2:T(8,128)(2,1)S(1)}, bf16[50,128,1]{1,0,2:T(8,128)(2,1)S(1)}, u32[]{:S(2)}, u32[]{:S(2)}) collective-permute-start(bf16[50,128,1]{1,0,2:T(8,128)(2,1)S(1)} %copy.19), channel_id=1, source_target_pairs={{8,0},{16,8},{24,16},{9,1},{17,9},{25,17},{10,2},{18,10},{26,18},{... | collective-permute-start | bytes 38408 | tf_op jit(solution)/shard_map/ppermute | solution.py:22
  62.5 42.3 %copy-start = (f32[34,130,258]{2,0,1:T(8,128)}, f32[34,130,258]{2,0,1:T(8,128)S(1)}, u32[]{:S(2)}) copy-start(f32[34,130,258]{2,0,1:T(8,128)S(1)} %pad_convert_fusion) | copy-start | bytes 13684324
  73.1 5.2 %slice-start.3 = ((s8[5242880]{0:T(1024)(128)(4,1)}), s8[1048576]{0:T(1024)(128)(4,1)S(1)}, s32[]{:S(2)}) async-start(s8[5242880]{0:T(1024)(128)(4,1)} %bitcast.79), calls=%async_computation.5 | async-start | bytes 2097152
  78.1 11.3 %copy-start.2 = (f32[1,32,128,256]{3,1,2,0:T(8,128)}, f32[1,32,128,256]{3,1,2,0:T(8,128)S(1)}, u32[]{:S(2)}) copy-start(f32[1,32,128,256]{3,1,2,0:T(8,128)S(1)} %fusion.26) | copy-start | bytes 12582916
  78.4 11.1 %copy-start.19 = (f32[128,3,3,256]{3,0,2,1:T(8,128)S(1)}, f32[128,3,3,256]{3,0,2,1:T(8,128)}, u32[]{:S(2)}) copy-start(f32[128,3,3,256]{3,0,2,1:T(8,128)} %fusion.55) | copy-start | bytes 3538948
  104.8 48.7 %copy-start.10 = (bf16[32,128,256]{2,1,0:T(8,128)(2,1)S(1)}, bf16[32,128,256]{2,1,0:T(8,128)(2,1)}, u32[]{:S(2)}) copy-start(bf16[32,128,256]{2,1,0:T(8,128)(2,1)} %param.5) | copy-start | bytes 6291460
  153.4 7.2 %copy-start.3 = (f32[1,32,128,256]{3,1,2,0:T(8,128)S(1)}, f32[1,32,128,256]{3,1,2,0:T(8,128)}, u32[]{:S(2)}) copy-start(f32[1,32,128,256]{3,1,2,0:T(8,128)} %copy-done.2) | copy-start | bytes 12582916
  153.4 7.2 %copy-start.5 = (f32[1,32,128,256]{3,1,2,0:T(8,128)S(1)}, f32[1,32,128,256]{3,1,2,0:T(8,128)}, u32[]{:S(2)}) copy-start(f32[1,32,128,256]{3,1,2,0:T(8,128)} %get-tuple-element.41) | copy-start | bytes 12582916
  153.5 8.1 %copy-start.7 = (f32[1,32,128,256]{3,1,2,0:T(8,128)S(1)}, f32[1,32,128,256]{3,1,2,0:T(8,128)}, u32[]{:S(2)}) copy-start(f32[1,32,128,256]{3,1,2,0:T(8,128)} %get-tuple-element.42) | copy-start | bytes 12582916
  170.5 342.1 %all-reduce.8.cloned.1.call-start = ((), (), s32[]{:S(2)}) async-start(), calls=%async_computation.1 | async-start | bytes 626688 | tf_op jit(solution)/shard_map/psum | solution.py:125
  303.1 16.6 %slice-start = ((s8[7987200]{0:T(1024)(128)(4,1)}), s8[4194304]{0:T(1024)(128)(4,1)S(1)}, s32[]{:S(2)}) async-start(s8[7987200]{0:T(1024)(128)(4,1)} %bitcast.77), calls=%async_computation.2 | async-start | bytes 8388608
  304.2 15.4 %slice-start.1 = ((s8[7987200]{0:T(1024)(128)(4,1)}), s8[3792896]{0:T(1024)(128)(4,1)S(1)}, s32[]{:S(2)}) async-start(s8[7987200]{0:T(1024)(128)(4,1)} %bitcast.77), calls=%async_computation.3 | async-start | bytes 7585792
  365.5 8.0 %copy-start.4 = (f32[1,32,128,256]{3,1,2,0:T(8,128)S(1)}, f32[1,32,128,256]{3,1,2,0:T(8,128)}, u32[]{:S(2)}) copy-start(f32[1,32,128,256]{3,1,2,0:T(8,128)} %copy-done.2) | copy-start | bytes 12582916
  365.5 8.0 %copy-start.6 = (f32[1,32,128,256]{3,1,2,0:T(8,128)S(1)}, f32[1,32,128,256]{3,1,2,0:T(8,128)}, u32[]{:S(2)}) copy-start(f32[1,32,128,256]{3,1,2,0:T(8,128)} %get-tuple-element.41) | copy-start | bytes 12582916
  365.5 8.1 %copy-start.8 = (f32[1,32,128,256]{3,1,2,0:T(8,128)S(1)}, f32[1,32,128,256]{3,1,2,0:T(8,128)}, u32[]{:S(2)}) copy-start(f32[1,32,128,256]{3,1,2,0:T(8,128)} %get-tuple-element.42) | copy-start | bytes 12582916
  373.5 6.6 %copy-start.1 = (f32[32,128,256]{2,0,1:T(8,128)}, f32[32,128,256]{2,0,1:T(8,128)S(1)}, u32[]{:S(2)}) copy-start(f32[32,128,256]{2,0,1:T(8,128)S(1)} %get-tuple-element.22) | copy-start | bytes 12582916
  427.4 85.3 %copy-start.16 = (f32[3,17,9,65]{3,0,2,1:T(4,128)S(1)}, f32[3,17,9,65]{3,0,2,1:T(4,128)}, u32[]{:S(2)}) copy-start(f32[3,17,9,65]{3,0,2,1:T(4,128)} %param.9) | copy-start | bytes 358024
  (6 other events, 11.7 us)
Sparse Core Ops, SparseCore 0:
  170.7 130.7 all-reduce.5
  382.7 129.8 all-reduce.7
where the time goes:
time: 532 us; the launch traced here: 523 us
  waiting for transfers between devices  209 us (39%)
  blocking collectives  127 us (24%)
  other arithmetic  62.1 us (12%)
  matrix products  49.8 us (9%)
  local copies, waits for them, and re-layouts  38.4 us (7%)
  between operations  25.2 us (5%)
  starting transfers between devices  11.4 us (2%)
    psum x2, waiting for transfers between devices, local(): lax.psum((whole, jnp.sum(residual * residual)[None]), ('grp', 'dev'))  209 us
    psum x2, blocking collectives, local(): lax.psum((jnp.sum(warped), jnp.sum(warped * warped)), ('grp', 'dev'))  82.4 us
    psum x1, blocking collectives, local(): lax.psum((whole, jnp.sum(residual * residual)[None]), ('grp', 'dev'))  44.8 us
    dot_general x2, matrix products, interpolate(): return jnp.einsum('ciyz,xi->cxyz', partial_y, hat_x, precision=highest)  30.7 us
    another operation x2, other arithmetic, gradients(): return jnp.stack([slope_x, slope_y, slope_z])  16.1 us
    unnamed x50, local copies, waits for them, and re-layouts  13.3 us
    dot_general x2, matrix products, restrict(): partial_x = jnp.einsum('cxyz,xi->ciyz', terms, hat_x, precision=highest)  12.9 us
    concatenate x2, other arithmetic, with_halo(): shard = jnp.concatenate([before, shard, after], axis=dim)  10.7 us
  transfers between devices with their start and end apart: 6, of which 3 were waited for; matrix products, arithmetic and copies ran while one was open for 5% of the time, Pallas kernels for 0%

commit v1 on v0

v1 whole, which is shorter than its diff:
```python
import functools

import jax
import jax.numpy as jnp
from jax import lax
from jax.experimental import pallas as pl
from jax.experimental.pallas import tpu as pltpu
from jax.sharding import PartitionSpec as P

E = 16
SMAX = 8
MARGIN = SMAX + 1
EPS = 1e-06
F32 = jnp.float32
BF16 = jnp.bfloat16
HIGHEST = lax.Precision.HIGHEST
MESH = pl.DeviceIdType.MESH


def iota(shape, dim):
    return lax.broadcasted_iota(jnp.int32, shape, dim)


def dot(a, b):
    return jnp.dot(a, b, preferred_element_type=F32)


def split_dot_left(a, b):
    high = a.astype(BF16)
    low = (a - high.astype(F32)).astype(BF16)
    return dot(high, b) + dot(low, b)


def split_dot_right(a, b):
    high = b.astype(BF16)
    low = (b - high.astype(F32)).astype(BF16)
    return dot(a, high) + dot(a, low)


def hat(distance):
    return jnp.maximum(1.0 - jnp.abs(distance).astype(F32) / E, 0.0)


def kernel(
    grps, devs, ref_hbm, def_hbm, faces, shifts, init, precond,
    disp, res_hbm, misfit,
    ref_v, wide, face_b, face_f, turned, target, pa, pb, pc, image, field, fine, nodes, bands, offs,
    slab, packs, stats, nbuf, gbuf, dbuf,
    sem_loc, sem_hs, sem_hr, sem_fs, sem_fr, sem_ss, sem_sr, sem_ns, sem_nr, sem_gs, sem_gr, sem_ds, sem_dr, sem_out,
):
    width, rows, depth = ref_v.shape
    nodes_y, nodes_z = init.shape[2:]
    total = grps * devs
    count = float(total * width * rows * depth)
    gi, di = lax.axis_index("grp"), lax.axis_index("dev")
    me = gi * devs + di

    def place(peer):
        return (peer // devs, lax.rem(peer, devs))

    def exists(dg, dd):
        g, d = gi + dg, di + dd
        return (g >= 0) & (g < grps) & (d >= 0) & (d < devs)

    def remote(src, dst, ss, rs, g, d):
        return pltpu.make_async_remote_copy(
            src_ref=src, dst_ref=dst, send_sem=ss, recv_sem=rs, device_id=(g, d), device_id_type=MESH
        )

    load_def = pltpu.make_async_copy(def_hbm, wide.at[pl.ds(MARGIN, width)], sem_loc.at[0])
    load_ref = pltpu.make_async_copy(ref_hbm, ref_v, sem_loc.at[1])
    load_def.start()
    load_ref.start()

    barrier = pltpu.get_barrier_semaphore()

    def greet(k, carry):
        pl.semaphore_signal(barrier, inc=1, device_id=place(lax.rem(me + k, total)), device_id_type=MESH)
        return carry

    lax.fori_loop(1, total, greet, 0)
    pl.semaphore_wait(barrier, total - 1)

    to_right = remote(
        def_hbm.at[pl.ds(width - MARGIN, MARGIN)], wide.at[pl.ds(0, MARGIN)],
        sem_hs.at[0], sem_hr.at[0], gi, di + 1,
    )
    to_left = remote(
        def_hbm.at[pl.ds(0, MARGIN)], wide.at[pl.ds(MARGIN + width, MARGIN)],
        sem_hs.at[1], sem_hr.at[1], gi, di - 1,
    )
    has_left, has_right = di > 0, di < devs - 1

    @pl.when(has_right)
    def _():
        to_right.start()

    @pl.when(has_left)
    def _():
        to_left.start()

    face_moves = []
    for dg in (1, -1):
        for dd in (-1, 0, 1):
            side = 0 if dg == 1 else 1
            slot = 1 - dd
            copy = remote(
                faces.at[1 - side], face_b.at[side, slot],
                sem_fs.at[side, slot], sem_fr.at[side, slot], gi + dg, di + dd,
            )
            face_moves.append((dg, dd, copy))

            @pl.when(exists(dg, dd))
            def _(copy=copy):
                copy.start()

            @pl.when(jnp.logical_not(exists(-dg, -dd)))
            def _(side=side, slot=slot):
                face_b[side, slot] = jnp.zeros((width, rows), BF16)

    @pl.when(jnp.logical_not(has_left))
    def _():
        wide[pl.ds(0, MARGIN)] = jnp.zeros((MARGIN, rows, depth), BF16)

    @pl.when(jnp.logical_not(has_right))
    def _():
        wide[pl.ds(MARGIN + width, MARGIN)] = jnp.zeros((MARGIN, rows, depth), BF16)

    k, j = iota((depth, 2 * depth), 0), iota((depth, 2 * depth), 1)
    is_d = j >= depth
    gap = k - jnp.where(is_d, j - depth, j)
    smooth_w = jnp.where(gap == 0, 4.0, jnp.where(jnp.abs(gap) == 1, 1.0, 0.0))
    differ_w = jnp.where(jnp.abs(gap) == 1, gap, 0).astype(F32)
    bands[...] = jnp.where(is_d, differ_w, smooth_w).astype(BF16)
    k, j = iota((128, 2 * depth), 0), iota((128, 2 * depth), 1)
    low = (j == 0) | (j == depth)
    high = (j == depth - 1) | (j == 2 * depth - 1)
    offs[...] = jnp.where(low, k, jnp.where(high, k - 64, -1))

    nodes[...] = jnp.zeros_like(nodes)
    z_of = iota((128, depth), 1) + gi * depth
    hat_up = hat(z_of - E * iota((128, depth), 0))
    hat_y = hat(iota((rows, 16), 0) - E * iota((rows, 16), 1))

    def expand():
        along_z = jnp.dot(nodes[...], hat_up, preferred_element_type=F32, precision=HIGHEST) * (1.0 / 72.0)
        for m in range(9):
            fine[m] = jnp.dot(
                hat_y, along_z[16 * m : 16 * m + 16], preferred_element_type=F32, precision=HIGHEST
            )

    for c in range(3):
        for n in range(3):
            m = 3 * c + n
            nodes[16 * m : 16 * m + nodes_y, 0:nodes_z] = init[c, 2 * di + n]
    expand()

    load_ref.wait()

    def convert(x, carry):
        s0, s1 = carry
        t = ref_v[x].astype(F32)
        target[x] = t
        t = t.reshape(rows // 8, 8, depth)
        return s0 + jnp.sum(t, axis=0), s1 + jnp.sum(t * t, axis=0)

    zero = jnp.zeros((8, depth), F32)
    sum_t, sum_tt = lax.fori_loop(0, width, convert, (zero, zero))

    load_def.wait()

    @pl.when(has_right)
    def _():
        to_right.wait_send()
        to_left.wait_recv()

    @pl.when(has_left)
    def _():
        to_left.wait_send()
        to_right.wait_recv()

    for dg, dd, copy in face_moves:

        @pl.when(exists(dg, dd))
        def _(copy=copy):
            copy.wait_send()

        @pl.when(exists(-dg, -dd))
        def _(copy=copy):
            copy.wait_recv()

    shift = shifts[0, 0]
    for side in range(2):
        for slot in range(3):
            face_f[side, pl.ds(slot * width, width)] = face_b[side, slot].astype(F32)
    low_rows = face_f[0, pl.ds(width - 1 + shift, 40)]
    high_rows = face_f[1, pl.ds(width - 1 + shift, 40)]
    gap_rows = jnp.zeros((24, rows), F32)
    stacked = jnp.concatenate([low_rows, gap_rows, high_rows, gap_rows], axis=0)
    turned[...] = jnp.transpose(stacked).astype(BF16)

    row = iota((rows, depth), 0)
    column = iota((128, 2 * depth), 1)
    sign = jnp.where(column == depth, -1.0, 1.0)

    def gradient(x, carry):
        plane = wide[x + shift + SMAX]
        pick = jnp.where(offs[...] == x, sign, 0.0).astype(BF16)
        both = dot(plane, bands[...]) + dot(turned[...], pick)
        sz, dz = both[:, :depth], both[:, depth:]
        s_prev = jnp.where(row == 0, 0.0, pltpu.roll(sz, 1, 0))
        s_next = jnp.where(row == rows - 1, 0.0, pltpu.roll(sz, rows - 1, 0))
        d_prev = jnp.where(row == 0, 0.0, pltpu.roll(dz, 1, 0))
        d_next = jnp.where(row == rows - 1, 0.0, pltpu.roll(dz, rows - 1, 0))
        pa[x] = s_prev + s_next + 4.0 * sz
        pb[x] = s_next - s_prev
        pc[x] = d_prev + d_next + 4.0 * dz
        image[x] = plane.astype(F32)
        return carry

    lax.fori_loop(0, width + 2, gradient, 0)

    tile = (8, 128)
    lanes = depth // 128
    chunks = (rows // 8) * lanes

    def chunk_at(q):
        return pl.ds(pl.multiple_of((q // lanes) * 8, 8), 8), pl.ds(pl.multiple_of(lax.rem(q, lanes) * 128, 128), 128)

    def finish(e, base, sums, ry, rz):
        for m, (s0, s1) in enumerate(sums):
            s1 = s1 * (1.0 / E)
            f = base + m
            if e == 1:
                field[3 * f + 2, ry, rz] = s1
                field[3 * f + 1, ry, rz] = s0 - s1
            else:
                field[3 * f + 1, ry, rz] += s1
                field[3 * f, ry, rz] = s0 - s1

    zt = jnp.zeros(tile, F32)

    def pass_one(e):
        def body(q, carry):
            sw, sww = carry
            ry, rz = chunk_at(q)
            here = [fine[3 * c + e + 1, ry, rz] for c in range(3)]
            step = [(here[c] - fine[3 * c + e, ry, rz]) * (1.0 / E) for c in range(3)]
            sums = [(zt, zt)] * 9
            top = E * e + E + 1
            a1, a2 = pa[top - 1, ry, rz], pa[top, ry, rz]
            b1, b2 = pb[top - 1, ry, rz], pb[top, ry, rz]
            c1, c2 = pc[top - 1, ry, rz], pc[top, ry, rz]
            for i in range(E - 1, -1, -1):
                x = E * e + i
                a0, b0, c0 = pa[x, ry, rz], pb[x, ry, rz], pc[x, ry, rz]
                slopes = (a2 - a0, b0 + b2 + 4.0 * b1, c0 + c2 + 4.0 * c1)
                a1, a2, b1, b2, c1, c2 = a0, a1, b0, b1, c0, c1
                pa[x + 2, ry, rz] = slopes[0]
                pb[x + 2, ry, rz] = slopes[1]
                pc[x + 2, ry, rz] = slopes[2]
                here = [here[c] - step[c] for c in range(3)]
                w = image[x + 1, ry, rz] + (here[0] * slopes[0] + here[1] * slopes[1] + here[2] * slopes[2])
                t = target[x, ry, rz]
                sw = sw + w
                sww = sww + w * w
                terms = [s * t for s in slopes] + list(slopes) + [s * w for s in slopes]
                if i > 0:
                    sums = [(s0 + f, s1 + (s0 + f)) for (s0, s1), f in zip(sums, terms)]
                else:
                    sums = [(s0 + f, s1) for (s0, s1), f in zip(sums, terms)]
            finish(e, 0, sums, ry, rz)
            return sw, sww

        return body

    sums = (zt, zt)
    for e in (1, 0):
        sums = lax.fori_loop(0, chunks, pass_one(e), sums)
    sum_w, sum_ww = sums

    lane = iota((1, 128), 1)

    def whole_sum(v):
        return jnp.sum(jnp.sum(v, axis=0, keepdims=True), axis=1, keepdims=True)

    def stat_copy(it, peer):
        g, d = place(peer)
        return (
            remote(stats.at[it, me], stats.at[it, me], sem_ss.at[it, peer], sem_sr.at[it, me], g, d),
            remote(stats.at[it, peer], stats.at[it, peer], sem_ss.at[it, peer], sem_sr.at[it, peer], g, d),
        )

    def send_stats(it, values):
        line = jnp.zeros((1, 128), F32)
        for r, v in enumerate(values):
            line = jnp.where(lane == r, whole_sum(v), line)
        stats[it, me] = line

        def go(k, carry):
            stat_copy(it, lax.rem(me + k, total))[0].start()
            return carry

        lax.fori_loop(1, total, go, 0)

    def take_stats(it, kinds):
        def go(k, carry):
            out, arrive = stat_copy(it, lax.rem(me + k, total))
            out.wait_send()
            arrive.wait_recv()
            return carry

        lax.fori_loop(1, total, go, 0)
        line = jnp.sum(stats[it], axis=0)
        return [jnp.sum(jnp.where(lane == r, line, 0.0), axis=1, keepdims=True) for r in range(kinds)]

    z_of_t = iota((depth, 128), 0) + gi * depth
    hat_down = hat(z_of_t - E * iota((depth, 128), 1)).astype(BF16)
    r_out, y_in = iota((32, rows), 0), iota((32, rows), 1)
    hat_rows = []
    for n in range(3):
        node = r_out - n * nodes_y
        inside = (node >= 0) & (node < nodes_y)
        hat_rows.append(jnp.where(inside, hat(y_in - E * node), 0.0).astype(BF16))

    def gather_nodes(f, carry):
        out = jnp.zeros((32, 128), F32)
        for n in range(3):
            along = split_dot_left(field[3 * f + n], hat_down)
            out = out + split_dot_right(hat_rows[n], along)
        packs[f] = out * (1.0 / 72.0)
        return carry

    send_stats(0, (sum_t, sum_tt, sum_w, sum_ww))
    lax.fori_loop(0, 9, gather_nodes, 0)
    st, stt, sw, sww = take_stats(0, 4)
    mean_ref = st / count
    var_ref = stt / count - mean_ref * mean_ref
    mean_1 = sw / count
    var_1 = sww / count - mean_1 * mean_1
    ratio_1 = jnp.sqrt((var_ref + EPS) / (var_1 + EPS))
    for c in range(3):
        slab[c] = packs[c] - mean_ref * packs[3 + c] - ratio_1 * (packs[6 + c] - mean_1 * packs[3 + c])

    near = [(dg, dd) for dg in (-1, 0, 1) for dd in (-1, 0, 1) if (dg, dd) != (0, 0)]
    moves = []
    for s, (dg, dd) in enumerate(near):
        slot = near.index((-dg, -dd))
        copy = remote(slab, nbuf.at[slot], sem_ns.at[slot], sem_nr.at[slot], gi + dg, di + dd)
        moves.append((dg, dd, slot, copy))

        @pl.when(exists(dg, dd))
        def _(copy=copy):
            copy.start()

        @pl.when(jnp.logical_not(exists(-dg, -dd)))
        def _(slot=slot):
            nbuf[slot] = jnp.zeros((3, 32, 128), F32)

    for dg, dd, slot, copy in moves:

        @pl.when(exists(dg, dd))
        def _(copy=copy):
            copy.wait_send()

        @pl.when(exists(-dg, -dd))
        def _(copy=copy):
            copy.wait_recv()

    def node_rows(block, n):
        return block[n * nodes_y : (n + 1) * nodes_y, 0:nodes_z]

    for c in range(3):
        same = slab[c]
        for dg in (-1, 1):
            same = same + nbuf[near.index((dg, 0)), c]
        left = jnp.zeros((32, 128), F32)
        right = jnp.zeros((32, 128), F32)
        for dg in (-1, 0, 1):
            left = left + nbuf[near.index((dg, -1)), c]
            right = right + nbuf[near.index((dg, 1)), c]
        for n in range(3):
            force = node_rows(same, n)
            if n == 0:
                force = force + node_rows(left, 2)
            if n == 2:
                force = force + node_rows(right, 0)
            m = 3 * c + n
            nodes[16 * m : 16 * m + nodes_y, 0:nodes_z] = init[c, 2 * di + n] + precond[c, 2 * di + n] * force
    expand()

    mean_1t, mean_rt, ratio_1t = (jnp.broadcast_to(v, tile) for v in (mean_1, mean_ref, ratio_1))

    def pass_two(e):
        def body(q, carry):
            sv, svv, see, sev = carry
            ry, rz = chunk_at(q)
            here = [fine[3 * c + e + 1, ry, rz] for c in range(3)]
            step = [(here[c] - fine[3 * c + e, ry, rz]) * (1.0 / E) for c in range(3)]
            sums = [(zt, zt)] * 3
            for i in range(E - 1, -1, -1):
                x = E * e + i
                slopes = (pa[x + 2, ry, rz], pb[x + 2, ry, rz], pc[x + 2, ry, rz])
                here = [here[c] - step[c] for c in range(3)]
                w = image[x + 1, ry, rz] + (here[0] * slopes[0] + here[1] * slopes[1] + here[2] * slopes[2])
                v = w - mean_1t
                image[x + 1, ry, rz] = v
                r = target[x, ry, rz] - mean_rt - ratio_1t * v
                sv = sv + v
                svv = svv + v * v
                see = see + r * r
                sev = sev + r * v
                terms = [s * v for s in slopes]
                if i > 0:
                    sums = [(s0 + f, s1 + (s0 + f)) for (s0, s1), f in zip(sums, terms)]
                else:
                    sums = [(s0 + f, s1) for (s0, s1), f in zip(sums, terms)]
            finish(e, 6, sums, ry, rz)
            return sv, svv, see, sev

        return body

    sums = (zt, zt, zt, zt)
    for e in (1, 0):
        sums = lax.fori_loop(0, chunks, pass_two(e), sums)
    send_stats(1, sums)
    lax.fori_loop(6, 9, gather_nodes, 0)
    sv, svv, see, sev = take_stats(1, 4)
    drift = sv / count
    var_2 = svv / count - drift * drift
    ratio_2 = jnp.sqrt((var_ref + EPS) / (var_2 + EPS))
    change = ratio_1 - ratio_2
    level = ratio_2 * drift
    squares = (
        see / count + change * change * (svv / count) + level * level
        + 2.0 * change * (sev / count) - 2.0 * level * ratio_1 * drift + 2.0 * change * level * drift
    )
    misfit[...] = jnp.sqrt(jnp.maximum(squares, 0.0))

    for c in range(3):
        second = packs[c] - mean_ref * packs[3 + c] - ratio_2 * (packs[6 + c] - drift * packs[3 + c])
        gbuf[gi, c] = slab[c] + second

    def over_grp(kk):
        peer = lax.rem(gi + kk, grps)
        return (
            remote(gbuf.at[gi], gbuf.at[gi], sem_gs.at[peer], sem_gr.at[gi], peer, di),
            remote(gbuf.at[peer], gbuf.at[peer], sem_gs.at[peer], sem_gr.at[peer], peer, di),
        )

    def over_dev(kk):
        peer = lax.rem(di + kk, devs)
        return (
            remote(dbuf.at[di], dbuf.at[di], sem_ds.at[peer], sem_dr.at[di], gi, peer),
            remote(dbuf.at[peer], dbuf.at[peer], sem_ds.at[peer], sem_dr.at[peer], gi, peer),
        )

    def start_all(make, size):
        def go(kk, carry):
            make(kk)[0].start()
            return carry

        lax.fori_loop(1, size, go, 0)

    def wait_all(make, size):
        def go(kk, carry):
            out, arrive = make(kk)
            out.wait_send()
            arrive.wait_recv()
            return carry

        lax.fori_loop(1, size, go, 0)

    start_all(over_grp, grps)

    offset = mean_ref - level

    def final(x, carry):
        target[x] = target[x] - offset - ratio_2 * image[x + 1]
        return carry

    half = width // 2
    outs = [
        pltpu.make_async_copy(target.at[pl.ds(h * half, half)], res_hbm.at[pl.ds(h * half, half)], sem_out.at[h])
        for h in range(2)
    ]
    lax.fori_loop(0, half, final, 0)
    outs[0].start()
    wait_all(over_grp, grps)
    dbuf[di] = jnp.sum(gbuf[...], axis=0)
    start_all(over_dev, devs)
    lax.fori_loop(half, width, final, 0)
    outs[1].start()
    wait_all(over_dev, devs)

    def place_pair(d, carry):
        for c in range(3):
            block = dbuf[d, c]
            before = dbuf[jnp.maximum(d - 1, 0), c]
            first = node_rows(block, 0) + jnp.where(d > 0, node_rows(before, 2), 0.0)
            disp[c, 2 * d] = init[c, 2 * d] + precond[c, 2 * d] * first
            disp[c, 2 * d + 1] = init[c, 2 * d + 1] + precond[c, 2 * d + 1] * node_rows(block, 1)
        return carry

    lax.fori_loop(0, devs, place_pair, 0)
    for c in range(3):
        last = node_rows(dbuf[devs - 1, c], 2)
        disp[c, 2 * devs] = init[c, 2 * devs] + precond[c, 2 * devs] * last
    outs[0].wait()
    outs[1].wait()


def local(ref_volume, def_volume, shifts, init_disp, precond):
    width, rows, depth = ref_volume.shape
    devs, grps = lax.axis_size("dev"), lax.axis_size("grp")
    total = grps * devs
    faces = jnp.stack([def_volume[:, :, 0], def_volume[:, :, depth - 1]])
    vmem = pl.BlockSpec(memory_space=pltpu.VMEM)
    hbm = pl.BlockSpec(memory_space=pl.ANY)
    dma = pltpu.SemaphoreType.DMA
    volume = pltpu.VMEM((width, rows, depth), F32)
    padded = pltpu.VMEM((width + 2, rows, depth), F32)
    disp, residual, misfit = pl.pallas_call(
        functools.partial(kernel, grps, devs),
        out_shape=(
            jax.ShapeDtypeStruct(init_disp.shape, F32),
            jax.ShapeDtypeStruct((width, rows, depth), F32),
            jax.ShapeDtypeStruct((1, 1), F32),
        ),
        in_specs=[hbm, hbm, vmem, pl.BlockSpec(memory_space=pltpu.SMEM), vmem, vmem],
        out_specs=(vmem, hbm, vmem),
        scratch_shapes=[
            pltpu.VMEM((width, rows, depth), BF16),
            pltpu.VMEM((width + 2 * MARGIN, rows, depth), BF16),
            pltpu.VMEM((2, 3, width, rows), BF16),
            pltpu.VMEM((2, 3 * width, rows), F32),
            pltpu.VMEM((rows, 128), BF16),
            volume,
            padded, padded, padded, padded,
            pltpu.VMEM((27, rows, depth), F32),
            pltpu.VMEM((9, rows, depth), F32),
            pltpu.VMEM((144, 128), F32),
            pltpu.VMEM((depth, 2 * depth), BF16),
            pltpu.VMEM((128, 2 * depth), jnp.int32),
            pltpu.VMEM((3, 32, 128), F32),
            pltpu.VMEM((9, 32, 128), F32),
            pltpu.VMEM((2, total, 1, 128), F32),
            pltpu.VMEM((8, 3, 32, 128), F32),
            pltpu.VMEM((grps, 3, 32, 128), F32),
            pltpu.VMEM((devs, 3, 32, 128), F32),
            dma((2,)), dma((2,)), dma((2,)), dma((2, 3)), dma((2, 3)),
            dma((2, total)), dma((2, total)), dma((8,)), dma((8,)),
            dma((grps,)), dma((grps,)), dma((devs,)), dma((devs,)), dma((2,)),
        ],
        compiler_params=pltpu.CompilerParams(
            collective_id=0, has_side_effects=True, vmem_limit_bytes=56 * 1024 * 1024
        ),
        cost_estimate=pl.CostEstimate(flops=10**9, bytes_accessed=10**7, transcendentals=0),
    )(ref_volume, def_volume, faces, shifts, init_disp, precond)
    return disp, residual, misfit[0, 0]


def solution(mesh):
    placed = (P("dev", None, "grp"), P("dev", None, "grp"), P("grp", "dev"), P(), P())
    return jax.shard_map(
        local,
        mesh=mesh,
        in_specs=placed,
        out_specs=(P(), P("dev", None, "grp"), P()),
        check_vma=False,
    )
```

time: 532 us -> 91.1 us (0.17); the launches traced: 523 us -> 90.7 us
  waiting for transfers between devices: 209 us -> 0 us
  blocking collectives: 127 us -> 0 us
  Pallas kernels: 0 us -> 74.2 us
  other arithmetic: 62.1 us -> 0.62 us
  matrix products: 49.8 us -> 0 us
  local copies, waits for them, and re-layouts: 38.4 us -> 12.8 us
  between operations: 25.2 us -> 3.05 us
  starting transfers between devices: 11.4 us -> 0 us
    psum x2 -> x0, waiting for transfers between devices: 209 us -> none  [local(): lax.psum((whole, jnp.sum(residual * residual)[None]), ('grp', 'dev'))]
    psum x3 -> x0, blocking collectives: 127 us -> none  [the longest x2 82.4 us: local(): lax.psum((jnp.sum(warped), jnp.sum(warped * warped)), ('grp', 'dev'))]
    pallas_call x0 -> x1, Pallas kernels: none -> 74.2 us  [local(): pl.pallas_call(functools.partial(kernel, grps, devs), out_shape=(jax.Shap...]
    dot_general x12 -> x0, matrix products: 49.8 us -> none  [the longest x2 30.7 us: interpolate(): return jnp.einsum('ciyz,xi->cxyz', partial_y, hat_x, precision=highest)]
    another operation x2 -> x1, other arithmetic: 16.1 us -> 0.62 us  [local(): faces = jnp.stack([def_volume[:, :, 0], def_volume[:, :, depth - 1]])]
    reduce_sum x4 -> x0, other arithmetic: 13.9 us -> none  [the longest x1 8 us: local(): jnp.sum(residual * residual)[None]]
    ppermute x4 -> x0, starting transfers between devices: 11.1 us -> none  [the longest x2 7.7 us: with_halo(): before = lax.ppermute(last, axis, up)]
    concatenate x2 -> x0, other arithmetic: 10.7 us -> none  [with_halo(): shard = jnp.concatenate([before, shard, after], axis=dim)]
  transfers between devices with their start and end apart: 6 -> 0, of which waited for: 3 -> 0; matrix products, arithmetic and copies ran while one was open for 5% -> 0% of each run, Pallas kernels for 0% -> 0%
where the time goes in v1:
time: 91.1 us; the launch traced here: 90.7 us
  Pallas kernels  74.2 us (81%)
  local copies, waits for them, and re-layouts  12.8 us (14%)
  between operations  3.05 us (3%)
    pallas_call x1, Pallas kernels, local(): pl.pallas_call(functools.partial(kernel, grps, devs), out_shape=(jax.Shap...  74.2 us
    unnamed x6, local copies, waits for them, and re-layouts  10.8 us
    slice x1, local copies, waits for them, and re-layouts, local(): faces = jnp.stack([def_volume[:, :, 0], def_volume[:, :, depth - 1]])  2.01 us

profile of v1, /device:TPU:1, one launch (start us, length us, event | category | flops | bytes accessed | tf_op | source)
XLA Modules:
  0.0 90.7 jit_solution(14308304599896585353)
XLA Ops:
  1.3 1.8 %copy.10.init = f32[3,17,9,65]{3,2,1,0:T(8,128)} copy(f32[3,17,9,65]{3,0,2,1:T(4,128)} %param.8) | data formatting | bytes 238680 | tf_op args[3]
  3.0 1.8 %copy.11.precond = f32[3,17,9,65]{3,2,1,0:T(8,128)} copy(f32[3,17,9,65]{3,0,2,1:T(4,128)} %param.9) | data formatting | bytes 238680 | tf_op args[4]
  4.8 2.0 %fusion = (bf16[32,128,1]{2,1,0:T(8,128)(2,1)S(1)}, bf16[32,128,1]{2,1,0:T(8,128)(2,1)S(1)}) fusion(bf16[32,128,256]{2,1,0:T(8,128)(2,1)} %def_hbm.1), kind=kLoop, calls=%fused_computation.1 | loop fusion | bytes 32768 | tf_op jit(solution)/shard_map/slice | solution.py:517
  6.8 0.4 copy.13
  7.2 0.4 copy.14
  7.6 0.6 pad_maximum_fusion.faces
  8.2 74.2 %shard_map.76 = (f32[3,17,9,65]{3,2,1,0:T(8,128)}, f32[32,128,256]{2,1,0:T(8,128)}, f32[1,1]{1,0:T(1,128)}) custom-call(bf16[32,128,256]{2,1,0:T(8,128)(2,1)} %ref_hbm.1, bf16[32,128,256]{2,1,0:T(8,128)(2,1)} %def_hbm.1, bf16[2,32,128]{2,1,0:T(8,128)(2,1)} %pad_maximum_fusion.faces, s32[1,1]{1,0:T(1,128)S(6)} %copy.17.shifts, f32[3,17,9,65]{3,2,1,0:T(8,128)} %copy.10.init, ...), custom_call_target="tpu_custom_call" | custom-call | flops 1000000000 | bytes 10000000 | tf_op jit(solution)/shard_map/pallas_call | solution.py:523
  82.5 1.8 %copy.12 = f32[3,17,9,65]{3,0,2,1:T(4,128)} copy(f32[3,17,9,65]{3,2,1,0:T(8,128)} %get-tuple-element.9) | data formatting | bytes 238680
  84.3 4.7 %copy.18 = f32[32,128,256]{2,1,0:T(8,128)} copy(f32[32,128,256]{2,1,0:T(8,128)} %get-tuple-element.18) | data formatting | bytes 8388608

commit v2 on v1

--- a/solution.py
+++ b/solution.py
@@ -10,6 +10,7 @@
 E = 16
 SMAX = 8
 MARGIN = SMAX + 1
+SPAN = 32
 EPS = 1e-06
 F32 = jnp.float32
 BF16 = jnp.bfloat16
@@ -42,14 +43,14 @@
 
 
 def kernel(
-    grps, devs, ref_hbm, def_hbm, faces, shifts, init, precond,
-    disp, res_hbm, misfit,
-    ref_v, wide, face_b, face_f, turned, target, pa, pb, pc, image, field, fine, nodes, bands, offs,
-    slab, packs, stats, nbuf, gbuf, dbuf,
+    grps, devs, ref_hbm, def_hbm, shifts, init, precond,
+    disp, centred_hbm, scalars,
+    ref_v, wide, faces, face_n, face_b, face_f, turned, target, pa, pb, pc, image, field, fine, nodes, bands, offs,
+    downs, slab, packs, stats, nbuf, gbuf, dbuf,
     sem_loc, sem_hs, sem_hr, sem_fs, sem_fr, sem_ss, sem_sr, sem_ns, sem_nr, sem_gs, sem_gr, sem_ds, sem_dr, sem_out,
 ):
     width, rows, depth = ref_v.shape
-    nodes_y, nodes_z = init.shape[2:]
+    nodes_y, nodes_z = init.shape[1], init.shape[3]
     total = grps * devs
     count = float(total * width * rows * depth)
     gi, di = lax.axis_index("grp"), lax.axis_index("dev")
@@ -79,6 +80,22 @@
         return carry
 
     lax.fori_loop(1, total, greet, 0)
+    load_def.wait()
+    ends, at = iota((16, depth), 0), iota((16, depth), 1)
+    pick_ends = jnp.where(((ends == 0) & (at == 0)) | ((ends == 1) & (at == depth - 1)), 1.0, 0.0).astype(BF16)
+
+    def cut(q, carry):
+        for i in range(8):
+            x = 8 * q + i
+            both = lax.dot_general(
+                pick_ends, wide[MARGIN + x], (((1,), (1,)), ((), ())), preferred_element_type=F32
+            )
+            face_n[x] = both[0:2]
+        return carry
+
+    lax.fori_loop(0, width // 8, cut, 0)
+    for side in range(2):
+        faces[side] = face_n[:, side].astype(BF16)
     pl.semaphore_wait(barrier, total - 1)
 
     to_right = remote(
@@ -152,7 +169,7 @@
     for c in range(3):
         for n in range(3):
             m = 3 * c + n
-            nodes[16 * m : 16 * m + nodes_y, 0:nodes_z] = init[c, 2 * di + n]
+            nodes[16 * m : 16 * m + nodes_y, 0:nodes_z] = init[2 * di + n, :, c]
     expand()
 
     load_ref.wait()
@@ -167,7 +184,6 @@
     zero = jnp.zeros((8, depth), F32)
     sum_t, sum_tt = lax.fori_loop(0, width, convert, (zero, zero))
 
-    load_def.wait()
 
     @pl.when(has_right)
     def _():
@@ -314,8 +330,11 @@
         line = jnp.sum(stats[it], axis=0)
         return [jnp.sum(jnp.where(lane == r, line, 0.0), axis=1, keepdims=True) for r in range(kinds)]
 
-    z_of_t = iota((depth, 128), 0) + gi * depth
-    hat_down = hat(z_of_t - E * iota((depth, 128), 1)).astype(BF16)
+    lane_t = iota((depth, 128), 1)
+    local_node = lane_t % SPAN
+    hat_down = jnp.where(local_node <= depth // E, hat(iota((depth, 128), 0) - E * local_node), 0.0)
+    for c in range(3):
+        downs[c] = jnp.where(lane_t // SPAN == c, hat_down, 0.0).astype(BF16)
     r_out, y_in = iota((32, rows), 0), iota((32, rows), 1)
     hat_rows = []
     for n in range(3):
@@ -323,24 +342,25 @@
         inside = (node >= 0) & (node < nodes_y)
         hat_rows.append(jnp.where(inside, hat(y_in - E * node), 0.0).astype(BF16))
 
-    def gather_nodes(f, carry):
+    def gather_nodes(kind, carry):
         out = jnp.zeros((32, 128), F32)
         for n in range(3):
-            along = split_dot_left(field[3 * f + n], hat_down)
+            along = jnp.zeros((rows, 128), F32)
+            for c in range(3):
+                along = along + split_dot_left(field[9 * kind + 3 * c + n], downs[c])
             out = out + split_dot_right(hat_rows[n], along)
-        packs[f] = out * (1.0 / 72.0)
+        packs[kind] = out * (1.0 / 72.0)
         return carry
 
     send_stats(0, (sum_t, sum_tt, sum_w, sum_ww))
-    lax.fori_loop(0, 9, gather_nodes, 0)
+    lax.fori_loop(0, 3, gather_nodes, 0)
     st, stt, sw, sww = take_stats(0, 4)
     mean_ref = st / count
     var_ref = stt / count - mean_ref * mean_ref
     mean_1 = sw / count
     var_1 = sww / count - mean_1 * mean_1
     ratio_1 = jnp.sqrt((var_ref + EPS) / (var_1 + EPS))
-    for c in range(3):
-        slab[c] = packs[c] - mean_ref * packs[3 + c] - ratio_1 * (packs[6 + c] - mean_1 * packs[3 + c])
+    slab[...] = packs[0] - mean_ref * packs[1] - ratio_1 * (packs[2] - mean_1 * packs[1])
 
     near = [(dg, dd) for dg in (-1, 0, 1) for dd in (-1, 0, 1) if (dg, dd) != (0, 0)]
     moves = []
@@ -355,7 +375,7 @@
 
         @pl.when(jnp.logical_not(exists(-dg, -dd)))
         def _(slot=slot):
-            nbuf[slot] = jnp.zeros((3, 32, 128), F32)
+            nbuf[slot] = jnp.zeros((32, 128), F32)
 
     for dg, dd, slot, copy in moves:
 
@@ -370,15 +390,26 @@
     def node_rows(block, n):
         return block[n * nodes_y : (n + 1) * nodes_y, 0:nodes_z]
 
+    lane_b = iota((32, 128), 1) % SPAN
+    last = depth // E
+
+    def joined(middle, dd):
+        below = pltpu.roll(nbuf[near.index((-1, dd))], 128 - last, 1)
+        above = pltpu.roll(nbuf[near.index((1, dd))], last, 1)
+        return middle + jnp.where(lane_b == 0, below, jnp.where(lane_b == last, above, 0.0))
+
+    from_k, to_k = iota((128, 128), 0), iota((128, 128), 1) - gi * last
     for c in range(3):
-        same = slab[c]
-        for dg in (-1, 1):
-            same = same + nbuf[near.index((dg, 0)), c]
-        left = jnp.zeros((32, 128), F32)
-        right = jnp.zeros((32, 128), F32)
-        for dg in (-1, 0, 1):
-            left = left + nbuf[near.index((dg, -1)), c]
-            right = right + nbuf[near.index((dg, 1)), c]
+        fits = (to_k >= 0) & (to_k <= last) & (from_k == to_k + SPAN * c)
+        spread = jnp.where(fits, 1.0, 0.0)
+        same, left, right = (
+            jnp.dot(block, spread, preferred_element_type=F32, precision=HIGHEST)
+            for block in (
+                joined(slab[...], 0),
+                joined(nbuf[near.index((0, -1))], -1),
+                joined(nbuf[near.index((0, 1))], 1),
+            )
+        )
         for n in range(3):
             force = node_rows(same, n)
             if n == 0:
@@ -386,7 +417,7 @@
             if n == 2:
                 force = force + node_rows(right, 0)
             m = 3 * c + n
-            nodes[16 * m : 16 * m + nodes_y, 0:nodes_z] = init[c, 2 * di + n] + precond[c, 2 * di + n] * force
+            nodes[16 * m : 16 * m + nodes_y, 0:nodes_z] = init[2 * di + n, :, c] + precond[2 * di + n, :, c] * force
     expand()
 
     mean_1t, mean_rt, ratio_1t = (jnp.broadcast_to(v, tile) for v in (mean_1, mean_ref, ratio_1))
@@ -421,10 +452,16 @@
         return body
 
     sums = (zt, zt, zt, zt)
+    half = width // 2
+    outs = [
+        pltpu.make_async_copy(image.at[pl.ds(h * half + 1, half)], centred_hbm.at[pl.ds(h * half, half)], sem_out.at[h])
+        for h in range(2)
+    ]
     for e in (1, 0):
         sums = lax.fori_loop(0, chunks, pass_two(e), sums)
+        outs[e].start()
     send_stats(1, sums)
-    lax.fori_loop(6, 9, gather_nodes, 0)
+    gather_nodes(2, 0)
     sv, svv, see, sev = take_stats(1, 4)
     drift = sv / count
     var_2 = svv / count - drift * drift
@@ -435,11 +472,11 @@
         see / count + change * change * (svv / count) + level * level
         + 2.0 * change * (sev / count) - 2.0 * level * ratio_1 * drift + 2.0 * change * level * drift
     )
-    misfit[...] = jnp.sqrt(jnp.maximum(squares, 0.0))
-
-    for c in range(3):
-        second = packs[c] - mean_ref * packs[3 + c] - ratio_2 * (packs[6 + c] - drift * packs[3 + c])
-        gbuf[gi, c] = slab[c] + second
+    line = jnp.where(lane == 0, mean_ref - level, jnp.where(lane == 1, ratio_2, jnp.sqrt(jnp.maximum(squares, 0.0))))
+    scalars[...] = line
+
+    second = packs[0] - mean_ref * packs[1] - ratio_2 * (packs[2] - drift * packs[1])
+    dbuf[di] = slab[...] + second
 
     def over_grp(kk):
         peer = lax.rem(gi + kk, grps)
@@ -471,41 +508,27 @@
 
         lax.fori_loop(1, size, go, 0)
 
+    start_all(over_dev, devs)
+    wait_all(over_dev, devs)
+    for d in range(devs):
+        block = dbuf[d]
+        first = block[0:nodes_y]
+        if d > 0:
+            first = first + dbuf[d - 1][2 * nodes_y : 3 * nodes_y]
+        gbuf[gi, 2 * d * nodes_y : (2 * d + 1) * nodes_y] = first
+        gbuf[gi, (2 * d + 1) * nodes_y : (2 * d + 2) * nodes_y] = block[nodes_y : 2 * nodes_y]
+    gbuf[gi, 2 * devs * nodes_y : (2 * devs + 1) * nodes_y] = dbuf[devs - 1][2 * nodes_y : 3 * nodes_y]
+    gbuf[gi, (2 * devs + 1) * nodes_y :] = jnp.zeros((gbuf.shape[1] - (2 * devs + 1) * nodes_y, 128), F32)
     start_all(over_grp, grps)
-
-    offset = mean_ref - level
-
-    def final(x, carry):
-        target[x] = target[x] - offset - ratio_2 * image[x + 1]
-        return carry
-
-    half = width // 2
-    outs = [
-        pltpu.make_async_copy(target.at[pl.ds(h * half, half)], res_hbm.at[pl.ds(h * half, half)], sem_out.at[h])
-        for h in range(2)
-    ]
-    lax.fori_loop(0, half, final, 0)
-    outs[0].start()
     wait_all(over_grp, grps)
-    dbuf[di] = jnp.sum(gbuf[...], axis=0)
-    start_all(over_dev, devs)
-    lax.fori_loop(half, width, final, 0)
-    outs[1].start()
-    wait_all(over_dev, devs)
-
-    def place_pair(d, carry):
-        for c in range(3):
-            block = dbuf[d, c]
-            before = dbuf[jnp.maximum(d - 1, 0), c]
-            first = node_rows(block, 0) + jnp.where(d > 0, node_rows(before, 2), 0.0)
-            disp[c, 2 * d] = init[c, 2 * d] + precond[c, 2 * d] * first
-            disp[c, 2 * d + 1] = init[c, 2 * d + 1] + precond[c, 2 * d + 1] * node_rows(block, 1)
-        return carry
-
-    lax.fori_loop(0, devs, place_pair, 0)
+    spot = iota((gbuf.shape[1], 128), 1)
     for c in range(3):
-        last = node_rows(dbuf[devs - 1, c], 2)
-        disp[c, 2 * devs] = init[c, 2 * devs] + precond[c, 2 * devs] * last
+        force = jnp.zeros((gbuf.shape[1], 128), F32)
+        for g in range(grps):
+            moved = pltpu.roll(gbuf[g], (g * last - SPAN * c) % 128, 1)
+            force = force + jnp.where((spot >= g * last) & (spot <= (g + 1) * last), moved, 0.0)
+        for n in range(2 * devs + 1):
+            disp[n, :, c] = init[n, :, c] + precond[n, :, c] * force[n * nodes_y : (n + 1) * nodes_y, 0:nodes_z]
     outs[0].wait()
     outs[1].wait()
 
@@ -514,24 +537,27 @@
     width, rows, depth = ref_volume.shape
     devs, grps = lax.axis_size("dev"), lax.axis_size("grp")
     total = grps * devs
-    faces = jnp.stack([def_volume[:, :, 0], def_volume[:, :, depth - 1]])
+    gather_rows = -(-init_disp.shape[1] * init_disp.shape[2] // 8) * 8
+    init_t, precond_t = (jnp.transpose(a, (1, 2, 0, 3)) for a in (init_disp, precond))
     vmem = pl.BlockSpec(memory_space=pltpu.VMEM)
     hbm = pl.BlockSpec(memory_space=pl.ANY)
     dma = pltpu.SemaphoreType.DMA
     volume = pltpu.VMEM((width, rows, depth), F32)
     padded = pltpu.VMEM((width + 2, rows, depth), F32)
-    disp, residual, misfit = pl.pallas_call(
+    disp, centred, scalars = pl.pallas_call(
         functools.partial(kernel, grps, devs),
         out_shape=(
-            jax.ShapeDtypeStruct(init_disp.shape, F32),
+            jax.ShapeDtypeStruct(init_t.shape, F32),
             jax.ShapeDtypeStruct((width, rows, depth), F32),
-            jax.ShapeDtypeStruct((1, 1), F32),
+            jax.ShapeDtypeStruct((1, 128), F32),
         ),
-        in_specs=[hbm, hbm, vmem, pl.BlockSpec(memory_space=pltpu.SMEM), vmem, vmem],
+        in_specs=[hbm, hbm, pl.BlockSpec(memory_space=pltpu.SMEM), vmem, vmem],
         out_specs=(vmem, hbm, vmem),
         scratch_shapes=[
             pltpu.VMEM((width, rows, depth), BF16),
             pltpu.VMEM((width + 2 * MARGIN, rows, depth), BF16),
+            pltpu.VMEM((2, width, rows), BF16),
+            pltpu.VMEM((width, 2, rows), F32),
             pltpu.VMEM((2, 3, width, rows), BF16),
             pltpu.VMEM((2, 3 * width, rows), F32),
             pltpu.VMEM((rows, 128), BF16),
@@ -542,12 +568,13 @@
             pltpu.VMEM((144, 128), F32),
             pltpu.VMEM((depth, 2 * depth), BF16),
             pltpu.VMEM((128, 2 * depth), jnp.int32),
+            pltpu.VMEM((3, depth, 128), BF16),
+            pltpu.VMEM((32, 128), F32),
             pltpu.VMEM((3, 32, 128), F32),
-            pltpu.VMEM((9, 32, 128), F32),
             pltpu.VMEM((2, total, 1, 128), F32),
-            pltpu.VMEM((8, 3, 32, 128), F32),
-            pltpu.VMEM((grps, 3, 32, 128), F32),
-            pltpu.VMEM((devs, 3, 32, 128), F32),
+            pltpu.VMEM((8, 32, 128), F32),
+            pltpu.VMEM((grps, gather_rows, 128), F32),
+            pltpu.VMEM((devs, 32, 128), F32),
             dma((2,)), dma((2,)), dma((2,)), dma((2, 3)), dma((2, 3)),
             dma((2, total)), dma((2, total)), dma((8,)), dma((8,)),
             dma((grps,)), dma((grps,)), dma((devs,)), dma((devs,)), dma((2,)),
@@ -556,8 +583,10 @@
             collective_id=0, has_side_effects=True, vmem_limit_bytes=56 * 1024 * 1024
         ),
         cost_estimate=pl.CostEstimate(flops=10**9, bytes_accessed=10**7, transcendentals=0),
-    )(ref_volume, def_volume, faces, shifts, init_disp, precond)
-    return disp, residual, misfit[0, 0]
+    )(ref_volume, def_volume, shifts, init_t, precond_t)
+    offset, ratio, misfit = scalars[0, 0], scalars[0, 1], scalars[0, 2]
+    residual = ref_volume.astype(F32) - offset - ratio * centred
+    return jnp.transpose(disp, (2, 0, 1, 3)), residual, misfit
 
 
 def solution(mesh):

time: 91.1 us -> 78.1 us (0.86)
  local copies, waits for them, and re-layouts: 12.8 us -> 2.09 us
  Pallas kernels: 74.2 us -> 67.1 us
  other arithmetic: 0.62 us -> 6.39 us
  between operations: 3.05 us -> 1.44 us
    unnamed x6 -> x5, local copies, waits for them, and re-layouts: 10.8 us -> 0.73 us
    pallas_call x1, Pallas kernels: 74.2 us -> 67.1 us  [local(): pl.pallas_call(functools.partial(kernel, grps, devs), out_shape=(jax.Shap...]
    sub x0 -> x1, other arithmetic: none -> 6.39 us  [local(): residual = ref_volume.astype(F32) - offset - ratio * centred]
where the time goes in v2:
time: 78.1 us; the launch traced here: 77 us
  Pallas kernels  67.1 us (86%)
  other arithmetic  6.39 us (8%)
  local copies, waits for them, and re-layouts  2.09 us (3%)
  between operations  1.44 us (2%)
    pallas_call x1, Pallas kernels, local(): pl.pallas_call(functools.partial(kernel, grps, devs), out_shape=(jax.Shap...  67.1 us
    sub x1, other arithmetic, local(): residual = ref_volume.astype(F32) - offset - ratio * centred  6.39 us

profile of v2, /device:TPU:1, one launch (start us, length us, event | category | flops | bytes accessed | tf_op | source)
XLA Modules:
  0.0 77.0 jit_solution(7909645455680177604)
XLA Ops:
  0.6 0.0 copy-start
  1.4 67.1 %shard_map.76 = (f32[17,9,3,65]{3,2,1,0:T(4,128)}, f32[32,128,256]{2,1,0:T(8,128)}, f32[1,128]{1,0:T(1,128)}) custom-call(bf16[32,128,256]{2,1,0:T(8,128)(2,1)} %ref_hbm.1, bf16[32,128,256]{2,1,0:T(8,128)(2,1)} %def_hbm.1, s32[1,1]{1,0:T(1,128)S(6)} %copy.9.shifts, f32[17,9,3,65]{3,2,1,0:T(4,128)} %bitcast.7, f32[17,9,3,65]{3,2,1,0:T(4,128)} %bitcast.8), custom_call_target="tpu_custom_call" | custom-call | flops 1000000000 | bytes 10000000 | tf_op jit(solution)/shard_map/pallas_call | solution.py:547
  68.6 1.4 %fusion = (f32[1,1]{1,0:T(1,128)}, f32[1,1]{1,0:T(1,128)}, f32[1,1]{1,0:T(1,128)}) fusion(f32[1,128]{1,0:T(1,128)} %get-tuple-element.7), kind=kLoop, calls=%fused_computation.1 | loop fusion | bytes 24 | tf_op jit(solution)/shard_map/slice | solution.py:587
  69.9 0.0 copy-done
  69.9 0.0 copy-start.1
  69.9 6.4 %multiply_subtract_fusion = f32[32,128,256]{2,1,0:T(8,128)} fusion(f32[32,128,256]{2,1,0:T(8,128)} %get-tuple-element.8, bf16[32,128,256]{2,1,0:T(8,128)(2,1)S(1)} %copy-done, f32[]{:T(128)} %bitcast.4, f32[]{:T(128)} %bitcast.3), kind=kLoop, calls=%fused_computation | loop fusion | flops 4194304 | bytes 10485768 | tf_op jit(solution)/shard_map/sub | solution.py:588
  76.3 0.0 copy-done.1
  76.3 0.7 copy.10
Async XLA Ops:
  0.6 69.3 %copy-start = (bf16[32,128,256]{2,1,0:T(8,128)(2,1)S(1)}, bf16[32,128,256]{2,1,0:T(8,128)(2,1)}, u32[]{:S(2)}) copy-start(bf16[32,128,256]{2,1,0:T(8,128)(2,1)} %ref_hbm.1) | copy-start | bytes 6291460
  69.9 6.4 %copy-start.1 = (f32[17,9,3,65]{3,2,1,0:T(4,128)S(1)}, f32[17,9,3,65]{3,2,1,0:T(4,128)}, u32[]{:S(2)}) copy-start(f32[17,9,3,65]{3,2,1,0:T(4,128)} %get-tuple-element.6) | copy-start | bytes 358024
